TPU v7x, 32 devices: a whole 2x2x4 slice. The times are simulated.
32 devices in a mesh: blk: 4 (over z), uly: 8 (over y, x, core).
Axes of the slice: x: 2, y: 2, z: 4, core: 2. Of those that a mesh axis runs over, the one named last changes fastest.
Arguments:
- video_q: bfloat16 [4096, 2048], P(('blk', 'uly')), may hold values from -100 to 100
- video_k: bfloat16 [4096, 2048], P(('blk', 'uly')), may hold values from -100 to 100
- video_v: bfloat16 [4096, 2048], P(('blk', 'uly')), may hold values from -6 to 6
- text_q: bfloat16 [256, 2048], replicated, may hold values from -100 to 100
- text_k: bfloat16 [256, 2048], replicated, may hold values from -100 to 100
- text_v: bfloat16 [256, 2048], replicated, may hold values from -6 to 6
Outputs:
- video_out: bfloat16 [4096, 2048], P(('blk', 'uly'))
- text_out: bfloat16 [256, 2048], P(('blk', 'uly'))
All inputs are finite; a program needn't handle non-finite values.
Results may differ from a plain program's by a relative error of at most 0.0039.
Values may be sent and summed in bfloat16 or wider, within the bound.
A program may use at most 128 MiB of HBM per device.

v0:
```python
import jax
import jax.numpy as jnp
from jax import lax
from jax.sharding import PartitionSpec as P

HEAD_DIM = 128


def score_block(queries, key_part, score_scale):
    return (
        jnp.einsum("qhd,khd->hqk", queries, key_part, preferred_element_type=jnp.float32)
        * score_scale
    )


def first_state(queries, key_part, value_part, score_scale):
    scores = score_block(queries, key_part, score_scale)
    top_score = jnp.max(scores, axis=2)
    raised = jnp.exp(scores - top_score[:, :, None])
    denominator = jnp.sum(raised, axis=2)
    numerator = jnp.einsum(
        "hqk,khd->hqd", raised.astype(jnp.bfloat16), value_part, preferred_element_type=jnp.float32
    )
    return (numerator, top_score, denominator)


def absorb(softmax_state, queries, key_part, value_part, score_scale):
    numerator, top_score, denominator = softmax_state
    scores = score_block(queries, key_part, score_scale)
    new_top = jnp.maximum(top_score, jnp.max(scores, axis=2))
    factor = jnp.exp(top_score - new_top)
    raised = jnp.exp(scores - new_top[:, :, None])
    denominator = denominator * factor + jnp.sum(raised, axis=2)
    numerator = numerator * factor[:, :, None] + jnp.einsum(
        "hqk,khd->hqd", raised.astype(jnp.bfloat16), value_part, preferred_element_type=jnp.float32
    )
    return (numerator, new_top, denominator)


def fold_piece(softmax_state, key_piece, queries, score_scale, head_count):
    key_rows, value_rows = key_piece
    row_total = key_rows.shape[0]
    key_block = 2048
    turn_count = row_total // key_block

    def inner(turn_index, carried):
        row_start = turn_index * key_block
        key_part = lax.dynamic_slice_in_dim(key_rows, row_start, key_block, 0).reshape(
            key_block, head_count, HEAD_DIM
        )
        value_part = lax.dynamic_slice_in_dim(value_rows, row_start, key_block, 0).reshape(
            key_block, head_count, HEAD_DIM
        )
        return absorb(carried, queries, key_part, value_part, score_scale)

    return lax.fori_loop(0, turn_count, inner, softmax_state)


def joint_attention(queries, text_keys, text_values, folder):
    query_count = queries.shape[0]
    columns = queries.shape[1]
    head_count = columns // HEAD_DIM
    score_scale = HEAD_DIM ** (-0.5)
    shaped = queries.reshape(query_count, head_count, HEAD_DIM)
    start_state = first_state(
        shaped,
        text_keys.reshape(-1, head_count, HEAD_DIM),
        text_values.reshape(-1, head_count, HEAD_DIM),
        score_scale,
    )

    def absorb_piece(softmax_state, key_piece, row_start):
        return fold_piece(softmax_state, key_piece, shaped, score_scale, head_count)

    numerator, top_score, denominator = folder(absorb_piece, start_state)
    attended = numerator / denominator[:, :, None]
    return jnp.transpose(attended, (1, 0, 2)).reshape(query_count, columns).astype(jnp.bfloat16)


def per_device(video_q, video_k, video_v, text_q, text_k, text_v):
    columns_all = video_q.shape[1]
    text_count = text_q.shape[0]
    group_count = lax.axis_size("uly")
    my_group = lax.axis_index("uly")
    block_count = lax.axis_size("blk")
    my_block = lax.axis_index("blk")
    local_q, local_k, local_v = (
        lax.all_to_all(video_q, "uly", split_axis=1, concat_axis=0, tiled=True),
        lax.all_to_all(video_k, "uly", split_axis=1, concat_axis=0, tiled=True),
        lax.all_to_all(video_v, "uly", split_axis=1, concat_axis=0, tiled=True),
    )
    head_width = columns_all // group_count
    text_keys = lax.dynamic_slice_in_dim(text_k, my_group * head_width, head_width, 1)
    text_values = lax.dynamic_slice_in_dim(text_v, my_group * head_width, head_width, 1)
    text_share = text_count // block_count
    text_rows = lax.dynamic_slice_in_dim(text_q, my_block * text_share, text_share, 0)
    queries = jnp.concatenate(
        [local_q, lax.dynamic_slice_in_dim(text_rows, my_group * head_width, head_width, 1)], axis=0
    )

    def folder(absorb_piece, start_state):
        return absorb_piece(
            start_state,
            (
                lax.all_gather(local_k, "blk", axis=0, tiled=True),
                lax.all_gather(local_v, "blk", axis=0, tiled=True),
            ),
            jnp.int32(0),
        )

    output = joint_attention(queries, text_keys, text_values, folder)
    video_part = output[: local_q.shape[0]]
    text_mine = output[local_q.shape[0] :]
    video_out, text_out = (
        lax.all_to_all(video_part, "uly", split_axis=0, concat_axis=1, tiled=True),
        lax.all_to_all(text_mine, "uly", split_axis=0, concat_axis=1, tiled=True),
    )
    return (video_out, text_out)


def solution(mesh):
    return jax.shard_map(
        per_device,
        mesh=mesh,
        in_specs=(
            P(("blk", "uly"), None),
            P(("blk", "uly"), None),
            P(("blk", "uly"), None),
            P(),
            P(),
            P(),
        ),
        out_specs=(P(("blk", "uly"), None), P(("blk", "uly"), None)),
        check_vma=False,
    )
```

profile of v0, /device:TPU:0, one launch (start us, length us, event | category | flops | bytes accessed | tf_op | source)
XLA Modules:
  0.0 215.8 jit_solution(4783207066570355057)
XLA Ops:
  7.2 1.4 copy.64
  8.7 14.7 %all_to_all.92 = bf16[128,8,256]{0,2,1:T(8,128)(2,1)S(1)} all-to-all(bf16[128,8,256]{0,2,1:T(8,128)(2,1)S(1)} %bitcast.75), channel_id=1, replica_groups=mesh['blk'=4,'uly'=8] {'uly'}, dimensions={1} | all-to-all | bytes 1048576 | tf_op jit(solution)/shard_map/all_to_all | solution.py:89
  23.4 1.0 copy.65
  24.8 12.2 %all_to_all.93 = bf16[128,8,256]{0,2,1:T(8,128)(2,1)S(1)} all-to-all(bf16[128,8,256]{0,2,1:T(8,128)(2,1)S(1)} %bitcast.76), channel_id=1, replica_groups=mesh['blk'=4,'uly'=8] {'uly'}, dimensions={1} | all-to-all | bytes 1048576 | tf_op jit(solution)/shard_map/all_to_all | solution.py:90
  36.9 1.0 copy.67
  38.0 1.0 copy.56
  39.0 3.5 %all-to-all-start = ((bf16[128,8,256]{0,2,1:T(8,128)(2,1)}), bf16[128,8,256]{0,2,1:T(8,128)(2,1)S(1)}, u32[]{:S(2)}, u32[]{:S(2)}) async-start(bf16[128,8,256]{0,2,1:T(8,128)(2,1)} %bitcast.3), calls=%async_computation | async-start | bytes 1048576 | tf_op jit(solution)/shard_map/all_to_all | solution.py:88
  43.8 8.3 %all-to-all-done = bf16[128,8,256]{0,2,1:T(8,128)(2,1)S(1)} async-done(((bf16[128,8,256]{0,2,1:T(8,128)(2,1)}), bf16[128,8,256]{0,2,1:T(8,128)(2,1)S(1)}, u32[]{:S(2)}, u32[]{:S(2)}) %all-to-all-start) | async-done | bytes 524320 | tf_op jit(solution)/shard_map/all_to_all | solution.py:88
  55.1 1.6 fusion.11
  56.7 13.1 %all-gather.3.cloned.1.call-done = bf16[4096,256]{1,0:T(8,128)(2,1)} async-done(((bf16[1024,256]{1,0:T(8,128)(2,1)}), bf16[4096,256]{1,0:T(8,128)(2,1)}) %all-gather.3.cloned.1.call-update) | async-done | bytes 2097168 | tf_op jit(solution)/shard_map/all_gather | solution.py:105
  69.9 46.3 %all-gather.5.cloned.1.call-done = bf16[4096,256]{1,0:T(8,128)(2,1)} async-done(((bf16[1024,256]{1,0:T(8,128)(2,1)}), bf16[4096,256]{1,0:T(8,128)(2,1)}) %all-gather.5.cloned.1.call-update) | async-done | bytes 2097168 | tf_op jit(solution)/shard_map/all_gather | solution.py:106
  116.2 67.2 %while.17 = (s32[]{:T(128)}, f32[2,1088,128]{2,1,0:T(8,128)}, f32[2,1088]{1,0:T(2,128)S(1)}, f32[2,1088]{1,0:T(2,128)S(1)}, bf16[4096,256]{1,0:T(8,128)(2,1)}, /...) while((s32[]{:T(128)}, f32[2,1088,128]{2,1,0:T(8,128)}, ...), condition=%wide.region_5.0_spmd, body=%wide.region_2.0_spmd.sunk | while | flops 2317914368 | bytes 75800792 | solution.py:56
  116.2 2.6 %constant_dynamic-slice_fusion.5 = (bf16[2048,256]{1,0:T(8,128)(2,1)}, bf16[2048,256]{1,0:T(8,128)(2,1)S(1)}) fusion(bf16[4096,256]{1,0:T(8,128)(2,1)} %get-tuple-element.249, s32[]{:T(128)S(6)} %select_n.25, bf16[4096,256]{1,0:T(8,128)(2,1)} %get-tuple-element.247), kind=kLoop, calls=%fused_computation.9.clone.1 | loop fusion | bytes 4194308 | tf_op jit(solution)/shard_map/while/body/eval_jaxpr/dynamic_slice | solution.py:51
  118.8 1.5 copy.87
  120.3 1.4 copy.88
  121.7 10.0 %bitcast_reduce_fusion.2 = (f32[2,1088]{1,0:T(2,128)S(1)}, f32[2,2048,1088]{1,2,0:T(8,128)}) fusion(bf16[1088,2,128]{2,0,1:T(8,128)(2,1)} %get-tuple-element.248, bf16[2048,2,128]{0,2,1:T(8,128)(2,1)} %bitcast.68), kind=kOutput, calls=%fused_computation.1.clone.1 | convolution fusion | flops 1149761408 | bytes 19440128 | tf_op jit(solution)/shard_map/while/body/eval_jaxpr/qhd,khd->hqk/dot_general | solution.py:11
  131.7 9.2 %fusion.31 = f32[2,1088]{1,0:T(2,128)S(1)} fusion(f32[2,2048,1088]{1,2,0:T(8,128)} %get-tuple-element.217, f32[2,1088]{1,0:T(2,128)S(1)} %max.8), kind=kLoop, calls=%fused_computation.3.clone.1 | loop fusion | flops 13367168 | bytes 17843200 | tf_op jit(solution)/shard_map/while/body/eval_jaxpr/reduce_sum | solution.py:33
  140.9 7.8 %fusion.32 = f32[2,1088,128]{2,1,0:T(8,128)S(1)} fusion(bf16[2048,2,128]{0,2,1:T(8,128)(2,1)S(1)} %bitcast.67, f32[2,2048,1088]{1,2,0:T(8,128)} %get-tuple-element.217, f32[2,1088]{1,0:T(2,128)S(1)} %max.8, f32[2,1088,128]{2,1,0:T(8,128)S(1)} %copy-done.1, f32[2,1088]{1,0:T(2,128)S(1)} %get-tuple-element.219), kind=kOutput, calls=%fused_computation.6.clone.1 | convolution fusion | flops 1154777088 | bytes 21120000 | tf_op jit(solution)/shard_map/while/body/eval_jaxpr/hqk,khd->hqd/dot_general | solution.py:34
  148.8 1.0 copy-done.2
  149.8 2.6 %constant_dynamic-slice_fusion.5 = (bf16[2048,256]{1,0:T(8,128)(2,1)}, bf16[2048,256]{1,0:T(8,128)(2,1)S(1)}) fusion(bf16[4096,256]{1,0:T(8,128)(2,1)} %get-tuple-element.249, s32[]{:T(128)S(6)} %select_n.25, bf16[4096,256]{1,0:T(8,128)(2,1)} %get-tuple-element.247), kind=kLoop, calls=%fused_computation.9.clone.1 | loop fusion | bytes 4194308 | tf_op jit(solution)/shard_map/while/body/eval_jaxpr/dynamic_slice | solution.py:51
  152.4 1.5 copy.87
  153.9 1.4 copy.88
  155.3 10.0 %bitcast_reduce_fusion.2 = (f32[2,1088]{1,0:T(2,128)S(1)}, f32[2,2048,1088]{1,2,0:T(8,128)}) fusion(bf16[1088,2,128]{2,0,1:T(8,128)(2,1)} %get-tuple-element.248, bf16[2048,2,128]{0,2,1:T(8,128)(2,1)} %bitcast.68), kind=kOutput, calls=%fused_computation.1.clone.1 | convolution fusion | flops 1149761408 | bytes 19440128 | tf_op jit(solution)/shard_map/while/body/eval_jaxpr/qhd,khd->hqk/dot_general | solution.py:11
  165.3 9.2 %fusion.31 = f32[2,1088]{1,0:T(2,128)S(1)} fusion(f32[2,2048,1088]{1,2,0:T(8,128)} %get-tuple-element.217, f32[2,1088]{1,0:T(2,128)S(1)} %max.8), kind=kLoop, calls=%fused_computation.3.clone.1 | loop fusion | flops 13367168 | bytes 17843200 | tf_op jit(solution)/shard_map/while/body/eval_jaxpr/reduce_sum | solution.py:33
  174.6 7.8 %fusion.32 = f32[2,1088,128]{2,1,0:T(8,128)S(1)} fusion(bf16[2048,2,128]{0,2,1:T(8,128)(2,1)S(1)} %bitcast.67, f32[2,2048,1088]{1,2,0:T(8,128)} %get-tuple-element.217, f32[2,1088]{1,0:T(2,128)S(1)} %max.8, f32[2,1088,128]{2,1,0:T(8,128)S(1)} %copy-done.1, f32[2,1088]{1,0:T(2,128)S(1)} %get-tuple-element.219), kind=kOutput, calls=%fused_computation.6.clone.1 | convolution fusion | flops 1154777088 | bytes 21120000 | tf_op jit(solution)/shard_map/while/body/eval_jaxpr/hqk,khd->hqd/dot_general | solution.py:34
  182.4 1.0 copy-done.2
  183.4 1.6 fusion.14
  185.7 3.6 %all-to-all-start.4 = ((bf16[8,8,256]{2,1,0:T(8,128)(2,1)}), bf16[8,8,256]{2,1,0:T(8,128)(2,1)S(1)}, u32[]{:S(2)}, u32[]{:S(2)}) async-start(bf16[8,8,256]{2,1,0:T(8,128)(2,1)} %all_to_all.83), calls=%async_computation.4 | async-start | bytes 65536 | tf_op jit(solution)/shard_map/all_to_all | solution.py:116
  190.6 3.6 %all-to-all-done.4 = bf16[8,8,256]{2,1,0:T(8,128)(2,1)S(1)} async-done(((bf16[8,8,256]{2,1,0:T(8,128)(2,1)}), bf16[8,8,256]{2,1,0:T(8,128)(2,1)S(1)}, u32[]{:S(2)}, u32[]{:S(2)}) %all-to-all-start.4) | async-done | bytes 32800 | tf_op jit(solution)/shard_map/all_to_all | solution.py:116
  194.2 3.5 %all-to-all-start.3 = ((bf16[8,128,256]{1,2,0:T(8,128)(2,1)}), bf16[8,128,256]{1,2,0:T(8,128)(2,1)S(1)}, u32[]{:S(2)}, u32[]{:S(2)}) async-start(bf16[8,128,256]{1,2,0:T(8,128)(2,1)} %copy.71), calls=%async_computation.3 | async-start | bytes 1048576 | tf_op jit(solution)/shard_map/all_to_all | solution.py:115
  197.7 9.7 %all-to-all-done.3 = bf16[8,128,256]{1,2,0:T(8,128)(2,1)S(1)} async-done(((bf16[8,128,256]{1,2,0:T(8,128)(2,1)}), bf16[8,128,256]{1,2,0:T(8,128)(2,1)S(1)}, u32[]{:S(2)}, u32[]{:S(2)}) %all-to-all-start.3) | async-done | bytes 524320 | tf_op jit(solution)/shard_map/all_to_all | solution.py:115
  207.3 1.0 copy.73
  (41 shorter events, 7.3 us)
Async XLA Ops:
  7.2 36.5 %copy-start = (bf16[256,2048]{1,0:T(8,128)(2,1)S(1)}, bf16[256,2048]{1,0:T(8,128)(2,1)}, u32[]{:S(2)}) copy-start(bf16[256,2048]{1,0:T(8,128)(2,1)} %param.11) | copy-start | bytes 3145732
  7.2 17.3 %copy-start.3 = (bf16[128,2048]{1,0:T(8,128)(2,1)S(1)}, bf16[128,2048]{1,0:T(8,128)(2,1)}, u32[]{:S(2)}) copy-start(bf16[128,2048]{1,0:T(8,128)(2,1)} %param.10) | copy-start | bytes 1572868
  7.2 62.7 %all-gather.3.cloned.1.call-start = ((), (), s32[]{:S(2)}) async-start(), calls=%async_computation.5 | async-start | bytes 2621440 | tf_op jit(solution)/shard_map/all_gather | solution.py:105
  24.4 13.6 %copy-start.4 = (bf16[128,2048]{1,0:T(8,128)(2,1)S(1)}, bf16[128,2048]{1,0:T(8,128)(2,1)}, u32[]{:S(2)}) copy-start(bf16[128,2048]{1,0:T(8,128)(2,1)} %param.8) | copy-start | bytes 1572868
  24.4 91.7 %all-gather.5.cloned.1.call-start = ((), (), s32[]{:S(2)}) async-start(), calls=%async_computation.6 | async-start | bytes 2621440 | tf_op jit(solution)/shard_map/all_gather | solution.py:106
  39.0 13.2 %all-to-all-start = ((bf16[128,8,256]{0,2,1:T(8,128)(2,1)}), bf16[128,8,256]{0,2,1:T(8,128)(2,1)S(1)}, u32[]{:S(2)}, u32[]{:S(2)}) async-start(bf16[128,8,256]{0,2,1:T(8,128)(2,1)} %bitcast.3), calls=%async_computation | async-start | bytes 1048576 | tf_op jit(solution)/shard_map/all_to_all | solution.py:88
  131.7 9.2 %copy-start.1 = (f32[2,1088,128]{2,1,0:T(8,128)S(1)}, f32[2,1088,128]{2,1,0:T(8,128)}, u32[]{:S(2)}) copy-start(f32[2,1088,128]{2,1,0:T(8,128)} %get-tuple-element.233) | copy-start | bytes 3342340 | tf_op jit(solution)/shard_map/while
  148.7 1.0 copy-start.2
  165.3 9.2 %copy-start.1 = (f32[2,1088,128]{2,1,0:T(8,128)S(1)}, f32[2,1088,128]{2,1,0:T(8,128)}, u32[]{:S(2)}) copy-start(f32[2,1088,128]{2,1,0:T(8,128)} %get-tuple-element.233) | copy-start | bytes 3342340 | tf_op jit(solution)/shard_map/while
  182.3 1.0 copy-start.2
  185.7 8.5 %all-to-all-start.4 = ((bf16[8,8,256]{2,1,0:T(8,128)(2,1)}), bf16[8,8,256]{2,1,0:T(8,128)(2,1)S(1)}, u32[]{:S(2)}, u32[]{:S(2)}) async-start(bf16[8,8,256]{2,1,0:T(8,128)(2,1)} %all_to_all.83), calls=%async_computation.4 | async-start | bytes 65536 | tf_op jit(solution)/shard_map/all_to_all | solution.py:116
  194.2 13.2 %all-to-all-start.3 = ((bf16[8,128,256]{1,2,0:T(8,128)(2,1)}), bf16[8,128,256]{1,2,0:T(8,128)(2,1)S(1)}, u32[]{:S(2)}, u32[]{:S(2)}) async-start(bf16[8,128,256]{1,2,0:T(8,128)(2,1)} %copy.71), calls=%async_computation.3 | async-start | bytes 1048576 | tf_op jit(solution)/shard_map/all_to_all | solution.py:115
Sparse Core Ops, SparseCore 0:
  24.6 45.2 all-gather.2
  71.4 44.6 all-gather.4
where the time goes:
time: 216 us
  waiting for transfers between devices  81.1 us (38%)
  matrix products  37.7 us (17%)
  blocking collectives  26.9 us (12%)
  local copies, waits for them, and re-layouts  23.6 us (11%)
  other arithmetic  21.6 us (10%)
  between operations  14.2 us (7%)
  starting transfers between devices  10.7 us (5%)
    all_gather x1, waiting for transfers between devices, folder(): lax.all_gather(local_v, 'blk', axis=0, tiled=True)  46.3 us
    dot_general x3, matrix products, score_block(): jnp.einsum('qhd,khd->hqk', queries, key_part, preferred_element_type=jnp....  20.5 us
    reduce_sum x2, other arithmetic, absorb(): denominator = denominator * factor + jnp.sum(raised, axis=2)  18.4 us
    dot_general x2, matrix products, absorb(): jnp.einsum('hqk,khd->hqd', raised.astype(jnp.bfloat16), value_part, prefe...  15.6 us
    all_to_all x1, blocking collectives, per_device(): lax.all_to_all(video_k, 'uly', split_axis=1, concat_axis=0, tiled=True)  14.7 us
    all_gather x1, waiting for transfers between devices, folder(): lax.all_gather(local_k, 'blk', axis=0, tiled=True)  13.1 us
    all_to_all x1, blocking collectives, per_device(): lax.all_to_all(video_v, 'uly', split_axis=1, concat_axis=0, tiled=True)  12.2 us
    all_to_all x1, waiting for transfers between devices, per_device(): lax.all_to_all(video_part, 'uly', split_axis=0, concat_axis=1, tiled=True)  9.68 us
  transfers between devices with their start and end apart: 5, of which 5 were waited for; matrix products, arithmetic and copies ran while one was open for 4% of the time, Pallas kernels for 0%

commit v1 on v0

v1 whole, which is shorter than its diff:
```python
import functools
import math

import jax
import jax.numpy as jnp
from jax import lax
from jax.experimental import pallas as pl
from jax.experimental.pallas import tpu as pltpu
from jax.sharding import PartitionSpec as P

HEAD_DIM = 128
CORES = 2
MESH = pl.DeviceIdType.MESH
EXPONENT_SCALE = HEAD_DIM ** (-0.5) * math.log2(math.e)


def chunk_bounds(total, width):
    count = max(total // width, 1)
    starts = [i * width for i in range(count)]
    return [(s, (total if i == count - 1 else starts[i + 1]) - s) for i, s in enumerate(starts)]


def score(queries, keys):
    return lax.dot_general(
        queries, keys, (((1,), (1,)), ((), ())), preferred_element_type=jnp.float32
    )


def weigh(raised, values):
    ones = jnp.ones(values.shape, values.dtype)
    return jnp.dot(
        raised, jnp.concatenate([values, ones], axis=1), preferred_element_type=jnp.float32
    )


def attend(queries, k_ref, v_ref, key_width):
    rows = queries.shape[0]
    key_count = k_ref.shape[0]

    def absorb(state, keys, values):
        top, total = state
        scores = score(queries, keys)
        part_top = jnp.max(scores, axis=1, keepdims=True)
        new_top = part_top if top is None else jnp.maximum(top, part_top)
        raised = jnp.exp2((scores - new_top) * EXPONENT_SCALE)
        part = weigh(raised.astype(jnp.bfloat16), values)
        if top is not None:
            part = total * jnp.exp2((top - new_top) * EXPONENT_SCALE) + part
        return new_top, part

    bounds = chunk_bounds(key_count, key_width)
    if len(bounds) <= 8:
        state = (None, None)
        for start, width in bounds:
            state = absorb(
                state, k_ref[start : start + width, :], v_ref[start : start + width, :]
            )
    else:
        start, width = bounds[-1]
        state = absorb(
            (None, None), k_ref[start : start + width, :], v_ref[start : start + width, :]
        )

        def step(index, state):
            rows_here = pl.ds(pl.multiple_of(index * key_width, key_width), key_width)
            return absorb(state, k_ref[rows_here, :], v_ref[rows_here, :])

        state = lax.fori_loop(0, len(bounds) - 1, step, state)
    total = state[1]
    return total[:, :HEAD_DIM] / total[:, HEAD_DIM:]


def kernel(
    blk_count, uly_count, key_width, group,
    vq, vk, vv, tq, tk, tv, vout, tout,
    kbuf, vbuf, qbuf, obuf, tqbuf, tsend, tin,
    local_sem, k_send, k_recv, v_send, v_recv, kf_send, kf_recv, vf_send, vf_recv,
    q_send, q_recv, o_send, o_recv, t_send, t_recv,
):
    rows = vq.shape[0]
    heads = vq.shape[1] // HEAD_DIM
    text = tq.shape[0]
    chips = blk_count * uly_count // CORES
    video_keys = chips * CORES * rows
    text_each = text // (chips * CORES)
    me = lax.axis_index("blk") * uly_count + lax.axis_index("uly")
    core = lax.rem(me, CORES)
    chip = me // CORES
    head = lax.rem(chip, heads)
    base = chip - head

    def device(to_chip, to_core):
        index = to_chip * CORES + to_core
        return (index // uly_count, lax.rem(index, uly_count))

    def columns(index):
        return pl.ds(pl.multiple_of(index * HEAD_DIM, HEAD_DIM), HEAD_DIM)

    def slot(k, of_core):
        return pl.ds(pl.multiple_of((k * CORES + of_core) * rows, rows), rows)

    def row_block(k):
        return pl.ds(pl.multiple_of(k * rows, rows), rows)

    def remote(src, dst, send, recv, target):
        return pltpu.make_async_remote_copy(
            src_ref=src, dst_ref=dst, send_sem=send, recv_sem=recv,
            device_id=target, device_id_type=MESH,
        )

    def kv_copies(k):
        to = lax.rem(chip + k, chips)
        where = columns(lax.rem(to, heads))
        return (
            remote(vk.at[:, where], kbuf.at[slot(k, core), :], k_send.at[k], k_recv.at[k], device(to, core)),
            remote(vv.at[:, where], vbuf.at[slot(k, core), :], v_send.at[k], v_recv.at[k], device(to, core)),
        )

    def forward_copies(k, of_core):
        part = slot(k, of_core)
        return (
            remote(kbuf.at[part, :], kbuf.at[part, :], kf_send.at[k], kf_recv.at[k], device(chip, 1 - core)),
            remote(vbuf.at[part, :], vbuf.at[part, :], vf_send.at[k], vf_recv.at[k], device(chip, 1 - core)),
        )

    def q_copy(k):
        to = lax.rem(head + k, heads)
        return remote(
            vq.at[:, columns(to)], qbuf.at[row_block(k), :], q_send.at[k], q_recv.at[k],
            device(base + to, core),
        )

    def o_copy(k):
        to = lax.rem(head - k + heads, heads)
        return remote(
            obuf.at[row_block(k), :], vout.at[:, columns(head)], o_send.at[k], o_recv.at[k],
            device(base + to, core),
        )

    def t_copy(k):
        to = lax.rem(head - k + heads, heads)
        return remote(tsend.at[k], tin.at[head], t_send.at[k], t_recv.at[k], device(base + to, core))

    text_rows = pl.ds(video_keys, text)
    own = [
        pltpu.make_async_copy(vk.at[:, columns(head)], kbuf.at[slot(0, core), :], local_sem.at[0]),
        pltpu.make_async_copy(vv.at[:, columns(head)], vbuf.at[slot(0, core), :], local_sem.at[1]),
        pltpu.make_async_copy(vq.at[:, columns(head)], qbuf.at[row_block(0), :], local_sem.at[2]),
        pltpu.make_async_copy(tq.at[:, columns(head)], tqbuf, local_sem.at[3]),
        pltpu.make_async_copy(tk.at[:, columns(head)], kbuf.at[text_rows, :], local_sem.at[4]),
        pltpu.make_async_copy(tv.at[:, columns(head)], vbuf.at[text_rows, :], local_sem.at[5]),
    ]
    for copy in own:
        copy.start()

    barrier = pltpu.get_barrier_semaphore()

    def greet(k, _):
        pl.semaphore_signal(
            barrier, inc=1, device_id=device(lax.rem(chip + k, chips), core), device_id_type=MESH
        )
        return 0

    lax.fori_loop(1, chips, greet, 0)
    pl.semaphore_signal(barrier, inc=1, device_id=device(chip, 1 - core), device_id_type=MESH)
    pl.semaphore_wait(barrier, chips)

    def send_kv(k, _):
        for copy in kv_copies(k):
            copy.start()
        return 0

    lax.fori_loop(1, chips, send_kv, 0)
    for copy in own:
        copy.wait()
    for copy in forward_copies(0, core):
        copy.start()

    def hand_on(k, _):
        for copy in kv_copies(k):
            copy.wait_recv()
        for copy in forward_copies(k, core):
            copy.start()
        if chips == heads:
            q_copy(k).start()
        else:
            pl.when(k < heads)(lambda: q_copy(k).start())
        return 0

    lax.fori_loop(1, chips, hand_on, 0)

    picked = heads * text_each
    shift = text_each.bit_length() - 1
    row = lax.broadcasted_iota(jnp.int32, (picked, text), 0)
    source = lax.broadcasted_iota(jnp.int32, (picked, text), 1)
    k_of = lax.shift_right_logical(row, shift)
    owner = head - k_of
    owner = base + jnp.where(owner < 0, owner + heads, owner)
    wanted = (owner * CORES + core) * text_each + (row - k_of * text_each)
    pick = jnp.where(source == wanted, 1.0, 0.0).astype(jnp.bfloat16)
    text_queries = jnp.dot(pick, tqbuf[...], preferred_element_type=jnp.float32).astype(jnp.bfloat16)

    def arrive(k, _):
        for copy in forward_copies(k, 1 - core):
            copy.wait_recv()
        return 0

    lax.fori_loop(0, chips, arrive, 0)

    attended = attend(text_queries, kbuf, vbuf, key_width)
    for k in range(heads):
        tsend[k, 0:text_each, :] = attended[k * text_each : (k + 1) * text_each, :]

    def send_text(k, _):
        t_copy(k).start()
        return 0

    lax.fori_loop(1, heads, send_text, 0)
    tin[head, :, :] = tsend[0, :, :]

    home = pltpu.make_async_copy(obuf.at[row_block(0), :], vout.at[:, columns(head)], local_sem.at[0])

    def block(b, _):
        for i in range(group):
            k = b * group + i
            if i == 0:
                pl.when(k > 0)(lambda: q_copy(k).wait_recv())
            else:
                q_copy(k).wait_recv()
        here = pl.ds(pl.multiple_of(b * group * rows, group * rows), group * rows)
        obuf[here, :] = attend(qbuf[here, :], kbuf, vbuf, key_width).astype(jnp.bfloat16)
        for i in range(group):
            k = b * group + i
            if i == 0:
                pl.when(k > 0)(lambda: o_copy(k).start())
                pl.when(k == 0)(lambda: home.start())
            else:
                o_copy(k).start()
        return 0

    lax.fori_loop(0, heads // group, block, 0)

    def finish(k, _):
        t_copy(k).wait()
        q_copy(k).wait_send()
        return 0

    lax.fori_loop(1, heads, finish, 0)
    for h in range(heads):
        tout[:, h * HEAD_DIM : (h + 1) * HEAD_DIM] = tin[h, 0:text_each, :].astype(jnp.bfloat16)
    home.wait()

    def finish_kv(k, _):
        for copy in kv_copies(k) + forward_copies(k, core):
            copy.wait_send()
        return 0

    for copy in forward_copies(0, core):
        copy.wait_send()
    lax.fori_loop(1, chips, finish_kv, 0)

    def finish_o(k, _):
        o_copy(k).wait()
        return 0

    lax.fori_loop(1, heads, finish_o, 0)


def per_device(blk_count, uly_count, video_q, video_k, video_v, text_q, text_k, text_v):
    rows, width = video_q.shape
    heads = width // HEAD_DIM
    text = text_q.shape[0]
    chips = blk_count * uly_count // CORES
    keys = chips * CORES * rows + text
    text_each = text // (chips * CORES)
    tile = max(text_each, 8)
    flops = 4 * (heads * rows + heads * text_each) * keys * HEAD_DIM
    dma = pltpu.SemaphoreType.DMA
    any_space = pl.BlockSpec(memory_space=pl.ANY)
    return pl.pallas_call(
        functools.partial(kernel, blk_count, uly_count, 1024, 2),
        out_shape=(
            jax.ShapeDtypeStruct((rows, width), jnp.bfloat16),
            jax.ShapeDtypeStruct((text_each, width), jnp.bfloat16),
        ),
        in_specs=[any_space] * 6,
        out_specs=(any_space, pl.BlockSpec(memory_space=pltpu.VMEM)),
        scratch_shapes=[
            pltpu.VMEM((keys, HEAD_DIM), jnp.bfloat16),
            pltpu.VMEM((keys, HEAD_DIM), jnp.bfloat16),
            pltpu.VMEM((heads * rows, HEAD_DIM), jnp.bfloat16),
            pltpu.VMEM((heads * rows, HEAD_DIM), jnp.bfloat16),
            pltpu.VMEM((text, HEAD_DIM), jnp.bfloat16),
            pltpu.VMEM((heads, tile, HEAD_DIM), jnp.float32),
            pltpu.VMEM((heads, tile, HEAD_DIM), jnp.float32),
            dma((6,)),
        ]
        + [dma((chips,))] * 8
        + [dma((heads,))] * 6,
        compiler_params=pltpu.CompilerParams(
            collective_id=0, has_side_effects=True, vmem_limit_bytes=56 * 1024 * 1024
        ),
        cost_estimate=pl.CostEstimate(
            flops=flops, bytes_accessed=8 * rows * width * 2, transcendentals=flops // (4 * HEAD_DIM)
        ),
    )(video_q, video_k, video_v, text_q, text_k, text_v)


def solution(mesh):
    rows = P(("blk", "uly"), None)
    return jax.shard_map(
        functools.partial(per_device, mesh.shape["blk"], mesh.shape["uly"]),
        mesh=mesh,
        in_specs=(rows, rows, rows, P(), P(), P()),
        out_specs=(rows, rows),
        check_vma=False,
    )
```

time: 216 us -> 70.9 us (0.33)
  waiting for transfers between devices: 81.1 us -> 0 us
  Pallas kernels: 0 us -> 67.6 us
  matrix products: 37.7 us -> 0 us
  blocking collectives: 26.9 us -> 0 us
  other arithmetic: 21.6 us -> 0 us
  local copies, waits for them, and re-layouts: 23.6 us -> 2.51 us
  between operations: 14.2 us -> 0.65 us
  starting transfers between devices: 10.7 us -> 0 us
    pallas_call x0 -> x1, Pallas kernels: none -> 67.6 us  [per_device(): pl.pallas_call(functools.partial(kernel, blk_count, uly_count, 1024, 2),...]
    all_gather x2 -> x0, waiting for transfers between devices: 59.4 us -> none  [the longest x1 46.3 us: folder(): lax.all_gather(local_v, 'blk', axis=0, tiled=True)]
    dot_general x6 -> x0, matrix products: 37.7 us -> none  [the longest x3 20.5 us: score_block(): jnp.einsum('qhd,khd->hqk', queries, key_part, preferred_element_type=jnp....]
    all_to_all x2 -> x0, blocking collectives: 26.9 us -> none  [the longest x1 14.7 us: per_device(): lax.all_to_all(video_k, 'uly', split_axis=1, concat_axis=0, tiled=True)]
    all_to_all x3 -> x0, waiting for transfers between devices: 21.6 us -> none  [the longest x1 9.68 us: per_device(): lax.all_to_all(video_part, 'uly', split_axis=0, concat_axis=1, tiled=True)]
    reduce_sum x3 -> x0, other arithmetic: 19.1 us -> none  [the longest x2 18.4 us: absorb(): denominator = denominator * factor + jnp.sum(raised, axis=2)]
    dynamic_slice x7 -> x0, local copies, waits for them, and re-layouts: 12.1 us -> none  [the longest x4 8.25 us: inner(): lax.dynamic_slice_in_dim(value_rows, row_start, key_block, 0)]
    all_to_all x3 -> x0, starting transfers between devices: 10.6 us -> none  [the longest x1 3.63 us: per_device(): lax.all_to_all(text_mine, 'uly', split_axis=0, concat_axis=1, tiled=True)]
  transfers between devices with their start and end apart: 5 -> 0, of which waited for: 5 -> 0; matrix products, arithmetic and copies ran while one was open for 4% -> 0% of each run, Pallas kernels for 0% -> 0%
where the time goes in v1:
time: 70.9 us; the launch traced here: 70.7 us
  Pallas kernels  67.6 us (95%)
  local copies, waits for them, and re-layouts  2.51 us (4%)
    pallas_call x1, Pallas kernels, per_device(): pl.pallas_call(functools.partial(kernel, blk_count, uly_count, 1024, 2),...  67.6 us
    unnamed x4, local copies, waits for them, and re-layouts  2.51 us

profile of v1, /device:TPU:0, one launch (start us, length us, event | category | flops | bytes accessed | tf_op | source)
XLA Modules:
  0.0 70.7 jit_solution(12958286230328363346)
XLA Ops:
  0.6 67.6 %shard_map.77 = (bf16[128,2048]{1,0:T(8,128)(2,1)}, bf16[8,2048]{1,0:T(8,128)(2,1)}) custom-call(bf16[128,2048]{1,0:T(8,128)(2,1)} %vq.1, bf16[128,2048]{1,0:T(8,128)(2,1)} %vk.1, bf16[128,2048]{1,0:T(8,128)(2,1)} %vv.1, bf16[256,2048]{1,0:T(8,128)(2,1)} %tq.1, bf16[256,2048]{1,0:T(8,128)(2,1)} %tk.1, bf16[256,2048]{1,0:T(8,128)(2,1)} %tv.1), custom_call_target="tpu_custom_call" | custom-call | flops 4848615424 | bytes 4194304 | tf_op jit(solution)/shard_map/pallas_call | solution.py:280
  68.2 0.0 copy-start
  68.2 1.9 %copy.10 = bf16[128,2048]{1,0:T(8,128)(2,1)} copy(bf16[128,2048]{1,0:T(8,128)(2,1)} %get-tuple-element.4) | data formatting | bytes 1048576
  70.1 0.0 copy-done
  70.1 0.6 copy.11
Async XLA Ops:
  68.2 1.9 %copy-start = (bf16[8,2048]{1,0:T(8,128)(2,1)S(1)}, bf16[8,2048]{1,0:T(8,128)(2,1)}, u32[]{:S(2)}) copy-start(bf16[8,2048]{1,0:T(8,128)(2,1)} %get-tuple-element.5) | copy-start | bytes 98308

commit v2 on v1

--- a/solution.py
+++ b/solution.py
@@ -18,6 +18,14 @@
     count = max(total // width, 1)
     starts = [i * width for i in range(count)]
     return [(s, (total if i == count - 1 else starts[i + 1]) - s) for i, s in enumerate(starts)]
+
+
+def pair(a, b, count):
+    total, bit = 0, 1
+    while bit < count:
+        total = total + lax.rem(a // bit + b // bit, 2) * bit
+        bit *= 2
+    return total
 
 
 def score(queries, keys):
@@ -109,7 +117,7 @@
         )
 
     def kv_copies(k):
-        to = lax.rem(chip + k, chips)
+        to = pair(chip, k, chips)
         where = columns(lax.rem(to, heads))
         return (
             remote(vk.at[:, where], kbuf.at[slot(k, core), :], k_send.at[k], k_recv.at[k], device(to, core)),
@@ -124,21 +132,21 @@
         )
 
     def q_copy(k):
-        to = lax.rem(head + k, heads)
+        to = pair(head, k, heads)
         return remote(
             vq.at[:, columns(to)], qbuf.at[row_block(k), :], q_send.at[k], q_recv.at[k],
             device(base + to, core),
         )
 
     def o_copy(k):
-        to = lax.rem(head - k + heads, heads)
+        to = pair(head, k, heads)
         return remote(
             obuf.at[row_block(k), :], vout.at[:, columns(head)], o_send.at[k], o_recv.at[k],
             device(base + to, core),
         )
 
     def t_copy(k):
-        to = lax.rem(head - k + heads, heads)
+        to = pair(head, k, heads)
         return remote(tsend.at[k], tin.at[head], t_send.at[k], t_recv.at[k], device(base + to, core))
 
     text_rows = pl.ds(video_keys, text)
@@ -157,7 +165,7 @@
 
     def greet(k, _):
         pl.semaphore_signal(
-            barrier, inc=1, device_id=device(lax.rem(chip + k, chips), core), device_id_type=MESH
+            barrier, inc=1, device_id=device(pair(chip, k, chips), core), device_id_type=MESH
         )
         return 0
 
@@ -165,7 +173,8 @@
     pl.semaphore_signal(barrier, inc=1, device_id=device(chip, 1 - core), device_id_type=MESH)
     pl.semaphore_wait(barrier, chips)
 
-    def send_kv(k, _):
+    def send_kv(j, _):
+        k = chips - j
         for copy in kv_copies(k):
             copy.start()
         return 0
@@ -176,7 +185,8 @@
     for copy in forward_copies(0, core):
         copy.start()
 
-    def hand_on(k, _):
+    def hand_on(j, _):
+        k = chips - j
         for copy in kv_copies(k):
             copy.wait_recv()
         for copy in forward_copies(k, core):
@@ -194,8 +204,7 @@
     row = lax.broadcasted_iota(jnp.int32, (picked, text), 0)
     source = lax.broadcasted_iota(jnp.int32, (picked, text), 1)
     k_of = lax.shift_right_logical(row, shift)
-    owner = head - k_of
-    owner = base + jnp.where(owner < 0, owner + heads, owner)
+    owner = base + lax.bitwise_xor(jnp.full_like(k_of, head), k_of)
     wanted = (owner * CORES + core) * text_each + (row - k_of * text_each)
     pick = jnp.where(source == wanted, 1.0, 0.0).astype(jnp.bfloat16)
     text_queries = jnp.dot(pick, tqbuf[...], preferred_element_type=jnp.float32).astype(jnp.bfloat16)
@@ -220,7 +229,8 @@
 
     home = pltpu.make_async_copy(obuf.at[row_block(0), :], vout.at[:, columns(head)], local_sem.at[0])
 
-    def block(b, _):
+    def block(step, _):
+        b = heads // group - 1 - step
         for i in range(group):
             k = b * group + i
             if i == 0:
@@ -278,7 +288,7 @@
     dma = pltpu.SemaphoreType.DMA
     any_space = pl.BlockSpec(memory_space=pl.ANY)
     return pl.pallas_call(
-        functools.partial(kernel, blk_count, uly_count, 1024, 2),
+        functools.partial(kernel, blk_count, uly_count, 2176, 4),
         out_shape=(
             jax.ShapeDtypeStruct((rows, width), jnp.bfloat16),
             jax.ShapeDtypeStruct((text_each, width), jnp.bfloat16),

time: 70.9 us -> 61.7 us (0.87)
  Pallas kernels: 67.6 us -> 58.4 us
    pallas_call x1, Pallas kernels: 67.6 us -> 58.4 us  [per_device(): pl.pallas_call(functools.partial(kernel, blk_count, uly_count, 2176, 4),...]
where the time goes in v2:
time: 61.7 us; the launch traced here: 61.6 us
  Pallas kernels  58.4 us (95%)
  local copies, waits for them, and re-layouts  2.51 us (4%)
  between operations  0.65 us (1%)
    pallas_call x1, Pallas kernels, per_device(): pl.pallas_call(functools.partial(kernel, blk_count, uly_count, 2176, 4),...  58.4 us
    unnamed x4, local copies, waits for them, and re-layouts  2.51 us

profile of v2, /device:TPU:0, one launch (start us, length us, event | category | flops | bytes accessed | tf_op | source)
XLA Modules:
  0.0 61.6 jit_solution(9625535201175340850)
XLA Ops:
  0.6 58.4 %shard_map.77 = (bf16[128,2048]{1,0:T(8,128)(2,1)}, bf16[8,2048]{1,0:T(8,128)(2,1)}) custom-call(bf16[128,2048]{1,0:T(8,128)(2,1)} %vq.1, bf16[128,2048]{1,0:T(8,128)(2,1)} %vk.1, bf16[128,2048]{1,0:T(8,128)(2,1)} %vv.1, bf16[256,2048]{1,0:T(8,128)(2,1)} %tq.1, bf16[256,2048]{1,0:T(8,128)(2,1)} %tk.1, bf16[256,2048]{1,0:T(8,128)(2,1)} %tv.1), custom_call_target="tpu_custom_call" | custom-call | flops 4848615424 | bytes 4194304 | tf_op jit(solution)/shard_map/pallas_call | solution.py:290
  59.1 0.0 copy-start
  59.1 1.9 %copy.10 = bf16[128,2048]{1,0:T(8,128)(2,1)} copy(bf16[128,2048]{1,0:T(8,128)(2,1)} %get-tuple-element.4) | data formatting | bytes 1048576
  61.0 0.0 copy-done
  61.0 0.6 copy.11
Async XLA Ops:
  59.1 1.9 %copy-start = (bf16[8,2048]{1,0:T(8,128)(2,1)S(1)}, bf16[8,2048]{1,0:T(8,128)(2,1)}, u32[]{:S(2)}) copy-start(bf16[8,2048]{1,0:T(8,128)(2,1)} %get-tuple-element.5) | copy-start | bytes 98308

commit v3 on v2

--- a/solution.py
+++ b/solution.py
@@ -276,6 +276,17 @@
     lax.fori_loop(1, heads, finish_o, 0)
 
 
+def hand_over(video, words, video_out, words_out, sem):
+    copies = [
+        pltpu.make_async_copy(video, video_out, sem.at[0]),
+        pltpu.make_async_copy(words, words_out, sem.at[1]),
+    ]
+    for copy in copies:
+        copy.start()
+    for copy in copies:
+        copy.wait()
+
+
 def per_device(blk_count, uly_count, video_q, video_k, video_v, text_q, text_k, text_v):
     rows, width = video_q.shape
     heads = width // HEAD_DIM
@@ -287,14 +298,14 @@
     flops = 4 * (heads * rows + heads * text_each) * keys * HEAD_DIM
     dma = pltpu.SemaphoreType.DMA
     any_space = pl.BlockSpec(memory_space=pl.ANY)
-    return pl.pallas_call(
+    video, words = pl.pallas_call(
         functools.partial(kernel, blk_count, uly_count, 2176, 4),
         out_shape=(
             jax.ShapeDtypeStruct((rows, width), jnp.bfloat16),
             jax.ShapeDtypeStruct((text_each, width), jnp.bfloat16),
         ),
         in_specs=[any_space] * 6,
-        out_specs=(any_space, pl.BlockSpec(memory_space=pltpu.VMEM)),
+        out_specs=(pl.BlockSpec(memory_space=pltpu.VMEM), pl.BlockSpec(memory_space=pltpu.VMEM)),
         scratch_shapes=[
             pltpu.VMEM((keys, HEAD_DIM), jnp.bfloat16),
             pltpu.VMEM((keys, HEAD_DIM), jnp.bfloat16),
@@ -314,6 +325,16 @@
             flops=flops, bytes_accessed=8 * rows * width * 2, transcendentals=flops // (4 * HEAD_DIM)
         ),
     )(video_q, video_k, video_v, text_q, text_k, text_v)
+    return pl.pallas_call(
+        hand_over,
+        out_shape=(
+            jax.ShapeDtypeStruct(video.shape, video.dtype),
+            jax.ShapeDtypeStruct(words.shape, words.dtype),
+        ),
+        in_specs=[pl.BlockSpec(memory_space=pltpu.VMEM)] * 2,
+        out_specs=(any_space,) * 2,
+        scratch_shapes=[dma((2,))],
+    )(video, words)
 
 
 def solution(mesh):

time: 61.7 us -> 61.2 us (level)
  local copies, waits for them, and re-layouts: 2.51 us -> 0 us
  Pallas kernels: 58.4 us -> 60.4 us
    unnamed x4 -> x0, local copies, waits for them, and re-layouts: 2.51 us -> none
    pallas_call x0 -> x1, Pallas kernels: none -> 1.86 us  [per_device(): pl.pallas_call(hand_over, out_shape=(jax.ShapeDtypeStruct(video.shape, vi...]
where the time goes in v3:
time: 61.2 us; the launch traced here: 61 us
  Pallas kernels  60.4 us (99%)
  between operations  0.64 us (1%)
    pallas_call x1, Pallas kernels, per_device(): pl.pallas_call(functools.partial(kernel, blk_count, uly_count, 2176, 4),...  58.5 us
    pallas_call x1, Pallas kernels, per_device(): pl.pallas_call(hand_over, out_shape=(jax.ShapeDtypeStruct(video.shape, vi...  1.86 us

profile of v3, /device:TPU:0, one launch (start us, length us, event | category | flops | bytes accessed | tf_op | source)
XLA Modules:
  0.0 61.0 jit_solution(6289611919513768177)
XLA Ops:
  0.6 58.5 %shard_map.77 = (bf16[128,2048]{1,0:T(8,128)(2,1)}, bf16[8,2048]{1,0:T(8,128)(2,1)}) custom-call(bf16[128,2048]{1,0:T(8,128)(2,1)} %vq.1, bf16[128,2048]{1,0:T(8,128)(2,1)} %vk.1, bf16[128,2048]{1,0:T(8,128)(2,1)} %vv.1, bf16[256,2048]{1,0:T(8,128)(2,1)} %tq.1, bf16[256,2048]{1,0:T(8,128)(2,1)} %tk.1, bf16[256,2048]{1,0:T(8,128)(2,1)} %tv.1), custom_call_target="tpu_custom_call" | custom-call | flops 4848615424 | bytes 4194304 | tf_op jit(solution)/shard_map/pallas_call | solution.py:301
  59.2 1.9 %shard_map.78 = (bf16[128,2048]{1,0:T(8,128)(2,1)}, bf16[8,2048]{1,0:T(8,128)(2,1)}) custom-call(bf16[128,2048]{1,0:T(8,128)(2,1)} %get-tuple-element.4.video, bf16[8,2048]{1,0:T(8,128)(2,1)} %get-tuple-element.5.words), custom_call_target="tpu_custom_call" | custom-call | tf_op jit(solution)/shard_map/pallas_call | solution.py:328
